TPU v7x, 512 devices: a whole 4x8x8 slice. The times are simulated.
512 devices in a mesh: cluster: 32 (over z_hi, x, core), blk: 16 (over y, z_lo).
Axes of the slice: x: 4, y: 8, z: 8 (z_hi: 4, z_lo: 2; z = z_hi * 2 + z_lo), core: 2. Of those that a mesh axis runs over, the one named last changes fastest.
Arguments:
- coeff: bfloat16 [1024, 8, 2048], P('cluster', None, 'blk'), may hold values from -0.375 to 0.375
- intersection: int32 [32, 32], replicated, may hold values from 0 to 1023, as said below
- basis_vals: bfloat16 [131072, 256], P(('cluster', 'blk')), may hold values from -6 to 6
- coulomb: bfloat16 [131072, 7, 256], P(('cluster', 'blk')), may hold values from -0.125 to 0.125
- reach: int32 [512], P(('cluster', 'blk')), may hold values from 0 to 3, as said below
Outputs:
- exchange_out: bfloat16 [131072, 2048], P(('cluster', 'blk'))
Inputs may be any that keep to these rules, and one draw needn't show every extreme that they name: `intersection`: each row lists 32 distinct atoms; atom a is owned by cluster a // 32; at most 2 atoms of one row have the same owner, and each row c holds exactly 2 atoms owned by cluster c. `reach`: some block reaches 3 and some block reaches 0.
All inputs are finite; a program needn't handle non-finite values.
Results may differ from a plain program's by a relative error of at most 0.0059.
Values may be sent and summed in bfloat16 or wider, within the bound.
A program may use at most 64 MiB of HBM per device.

v0:
```python
import jax
import jax.numpy as jnp
from jax import lax
from jax.sharding import PartitionSpec as P


def passed_along(value, axis, steps):
    count = lax.axis_size(axis)
    pairs = [(source, (source + steps) % count) for source in range(count)]
    return lax.ppermute(value, axis, pairs)


def block_term(local_vals, source, coul_tile, within, norm_factor):
    density = (
        lax.dot_general(
            local_vals, source, (((1,), (1,)), ((), ())), preferred_element_type=jnp.float32
        )
        * norm_factor
    )
    masked_tile = jnp.where(
        within, density * coul_tile.astype(jnp.float32), jnp.float32(0.0)
    ).astype(jnp.bfloat16)
    return jnp.dot(masked_tile, source, preferred_element_type=jnp.float32)


def on_device(coeff, intersection, basis_vals, coulomb, reach):
    num_clusters = lax.axis_size("cluster")
    my_cluster = lax.axis_index("cluster")
    atom_count = coeff.shape[0]
    list_len = intersection.shape[1]
    capacity = 2 * list_len // num_clusters
    num_funcs = coeff.shape[1]
    my_columns = coeff.shape[2]
    half_stops = (coulomb.shape[1] - 1) // 2
    owners = intersection // atom_count
    same_owner = owners[:, :, None] == owners[:, None, :]
    earlier = jnp.arange(list_len)[None, :] < jnp.arange(list_len)[:, None]
    slot_rank = jnp.sum(jnp.logical_and(same_owner, earlier[None, :, :]).astype(jnp.int32), axis=2)
    matches = jnp.logical_and(
        (owners == my_cluster)[:, :, None],
        slot_rank[:, :, None] == jnp.arange(capacity)[None, None, :],
    )
    local_atom = intersection - my_cluster * atom_count
    source_rows = jnp.sum(jnp.where(matches, local_atom[:, :, None], 0), axis=1)
    filled = jnp.any(matches, axis=1)
    outgoing = jnp.take(coeff, source_rows.reshape(-1), axis=0)
    outgoing = jnp.where(filled.reshape(-1)[:, None, None], outgoing, jnp.zeros_like(outgoing))
    outgoing = outgoing.reshape(num_clusters, capacity, num_funcs, my_columns)
    incoming = lax.all_to_all(outgoing, "cluster", split_axis=0, concat_axis=0, tiled=True)
    my_owners = lax.dynamic_index_in_dim(owners, my_cluster, 0, keepdims=False)
    my_ranks = lax.dynamic_index_in_dim(slot_rank, my_cluster, 0, keepdims=False)
    positions = my_owners * capacity + my_ranks
    needed = jnp.take(
        incoming.reshape(num_clusters * capacity, num_funcs * my_columns), positions, axis=0
    )
    needed = needed.reshape(list_len * num_funcs, my_columns)
    local_vals = jnp.dot(
        basis_vals,
        lax.all_gather(needed, "blk", axis=1, tiled=True),
        preferred_element_type=jnp.float32,
    ).astype(jnp.bfloat16)
    norm_factor = local_vals.shape[1] ** (-0.5)
    my_reach = reach[0]

    def term(source, offset):
        return block_term(
            local_vals,
            source,
            coulomb[:, offset + half_stops, :],
            abs(offset) <= my_reach,
            norm_factor,
        )

    accumulated = term(local_vals, 0)
    upward = local_vals
    downward = local_vals
    for stop_num in range(1, half_stops + 1):
        upward = passed_along(upward, "blk", -1)
        accumulated = accumulated + term(upward, stop_num)
        downward = passed_along(downward, "blk", 1)
        accumulated = accumulated + term(downward, -stop_num)
    return accumulated.astype(jnp.bfloat16)


def solution(mesh):
    return jax.shard_map(
        on_device,
        mesh=mesh,
        in_specs=(
            P("cluster", None, "blk"),
            P(),
            P(("cluster", "blk"), None),
            P(("cluster", "blk"), None, None),
            P(("cluster", "blk")),
        ),
        out_specs=P(("cluster", "blk"), None),
        check_vma=False,
    )
```

profile of v0, /device:TPU:114, one launch (start us, length us, event | category | flops | bytes accessed | tf_op | source)
XLA Modules:
  0.0 255.3 jit_solution(13018517774100364596)
XLA Ops:
  6.5 0.0 copy-start
  6.5 0.8 broadcast_compare_fusion
  7.3 0.7 broadcast_subtract_fusion
  8.0 0.8 convert_reduce_fusion
  8.8 0.1 select_reduce_fusion
  8.9 0.1 copy.8
  9.0 0.1 fusion.70
  9.2 0.1 reshape.131
  9.3 0.1 copy.7
  9.4 0.1 copy.6
  9.5 1.5 gather_fusion
  11.0 0.9 select_select_fusion
  11.8 12.6 %all-to-all-start = ((bf16[32,2,8,128]{3,2,1,0:T(8,128)(2,1)}), bf16[32,2,8,128]{3,2,1,0:T(8,128)(2,1)S(1)}, u32[]{:S(2)}, u32[]{:S(2)}) async-start(bf16[32,2,8,128]{3,2,1,0:T(8,128)(2,1)} %select_select_fusion), calls=%async_computation | async-start | bytes 262144 | tf_op jit(solution)/shard_map/all_to_all | solution.py:49
  24.4 0.0 all-gather.2.cloned.1.call-start
  24.5 0.1 broadcast_in_dim.66
  24.5 0.1 broadcast_in_dim.67
  24.7 9.1 %all-to-all-done = bf16[32,2,8,128]{3,2,1,0:T(8,128)(2,1)S(1)} async-done(((bf16[32,2,8,128]{3,2,1,0:T(8,128)(2,1)}), bf16[32,2,8,128]{3,2,1,0:T(8,128)(2,1)S(1)}, u32[]{:S(2)}, u32[]{:S(2)}) %all-to-all-start) | async-done | bytes 131104 | tf_op jit(solution)/shard_map/all_to_all | solution.py:49
  33.8 0.6 gather_fusion.1
  34.4 0.7 broadcast_select_fusion
  35.2 0.0 all-gather.2.cloned.1.call-update
  35.2 77.8 %all-gather.2.cloned.1.call-done = bf16[256,2048]{1,0:T(8,128)(2,1)} async-done(((bf16[256,128]{1,0:T(8,128)(2,1)}), bf16[256,2048]{1,0:T(8,128)(2,1)}) %all-gather.2.cloned.1.call-update) | async-done | bytes 1048592 | tf_op jit(solution)/shard_map/all_gather | solution.py:59
  113.0 0.0 copy-done
  113.0 1.7 convolution_convert_fusion
  114.7 1.9 collective-permute-start.1
  116.6 3.9 %collective-permute-start = (bf16[256,2048]{0,1:T(8,128)(2,1)S(1)}, bf16[256,2048]{0,1:T(8,128)(2,1)}, u32[]{:S(2)}, u32[]{:S(2)}) collective-permute-start(bf16[256,2048]{0,1:T(8,128)(2,1)S(1)} %bitcast.85), channel_id=1, source_target_pairs={{0,15},{1,0},{2,1},{3,2},{4,3},{5,4},{6,5},{7,6},{8,7},{9,8},{10,9... | collective-permute-start | bytes 3145736 | tf_op jit(solution)/shard_map/ppermute | solution.py:10
  120.5 41.8 %collective-permute-done.1 = bf16[256,2048]{0,1:T(8,128)(2,1)} collective-permute-done((bf16[256,2048]{0,1:T(8,128)(2,1)S(1)}, bf16[256,2048]{0,1:T(8,128)(2,1)}, u32[]{:S(2)}, u32[]{:S(2)}) %collective-permute-start.1) | collective-permute-done | bytes 1048608 | tf_op jit(solution)/shard_map/ppermute | solution.py:10
  162.3 1.9 collective-permute-start.3
  164.9 0.0 collective-permute-done
  164.9 3.9 %collective-permute-start.2 = (bf16[256,2048]{0,1:T(8,128)(2,1)}, bf16[256,2048]{0,1:T(8,128)(2,1)}, u32[]{:S(2)}, u32[]{:S(2)}) collective-permute-start(bf16[256,2048]{0,1:T(8,128)(2,1)} %collective-permute-done), channel_id=1, source_target_pairs={{0,15},{1,0},{2,1},{3,2},{4,3},{5,4},{6,5},{7,6},{8,7},{9,8},{10,9... | collective-permute-start | bytes 3145736 | tf_op jit(solution)/shard_map/ppermute | solution.py:10
  168.9 2.2 fusion.26
  171.1 4.4 %convolution_add_fusion.3 = f32[256,2048]{1,0:T(8,128)} fusion(f32[256,2048]{1,0:T(8,128)S(1)} %fusion.26, bf16[256,2048]{0,1:T(8,128)(2,1)} %collective-permute-done, bf16[2048,256]{1,0:T(8,128)(2,1)S(1)} %convolution_convert_fusion, bf16[256,7,256]{2,0,1:T(8,128)(2,1)} %param.8, pred[]{:T(512)} %bitcast.7), kind=kOutput, calls=%fused_computation.7 | convolution fusion | flops 537722880 | bytes 7471616 | tf_op jit(solution)/shard_map/dot_general | solution.py:23
  175.4 35.8 %collective-permute-done.3 = bf16[256,2048]{0,1:T(8,128)(2,1)} collective-permute-done((bf16[256,2048]{0,1:T(8,128)(2,1)}, bf16[256,2048]{0,1:T(8,128)(2,1)}, u32[]{:S(2)}, u32[]{:S(2)}) %collective-permute-start.3) | collective-permute-done | bytes 1048608 | tf_op jit(solution)/shard_map/ppermute | solution.py:10
  211.2 1.9 collective-permute-start.5
  213.1 4.9 %convolution_add_fusion.2 = f32[256,2048]{1,0:T(8,128)} fusion(f32[256,2048]{1,0:T(8,128)} %convolution_add_fusion.3, bf16[256,2048]{0,1:T(8,128)(2,1)} %collective-permute-done.1, bf16[2048,256]{1,0:T(8,128)(2,1)S(1)} %convolution_convert_fusion, bf16[256,7,256]{2,0,1:T(8,128)(2,1)} %param.8, pred[]{:T(512)} %bitcast.7), kind=kOutput, calls=%fused_computation.6 | convolution fusion | flops 537722880 | bytes 7471616 | tf_op jit(solution)/shard_map/dot_general | solution.py:23
  218.1 0.0 collective-permute-done.2
  218.1 3.9 %collective-permute-start.4 = (bf16[256,2048]{0,1:T(8,128)(2,1)}, bf16[256,2048]{0,1:T(8,128)(2,1)}, u32[]{:S(2)}, u32[]{:S(2)}) collective-permute-start(bf16[256,2048]{0,1:T(8,128)(2,1)} %collective-permute-done.2), channel_id=1, source_target_pairs={{0,15},{1,0},{2,1},{3,2},{4,3},{5,4},{6,5},{7,6},{8,7},{9,8},{10,9... | collective-permute-start | bytes 3145736 | tf_op jit(solution)/shard_map/ppermute | solution.py:10
  222.0 2.9 %fusion.25 = f32[256,2048]{1,0:T(8,128)S(1)} fusion(bf16[256,2048]{0,1:T(8,128)(2,1)} %collective-permute-done.3, bf16[2048,256]{1,0:T(8,128)(2,1)S(1)} %convolution_convert_fusion, bf16[256,7,256]{2,0,1:T(8,128)(2,1)} %param.8, pred[]{:T(512)} %bitcast.11), kind=kOutput, calls=%fused_computation.39 | convolution fusion | flops 537198592 | bytes 5374464 | tf_op jit(solution)/shard_map/dot_general | solution.py:23
  224.9 4.9 %fusion.1 = f32[256,2048]{1,0:T(8,128)} fusion(f32[256,2048]{1,0:T(8,128)S(1)} %fusion.25, f32[256,2048]{1,0:T(8,128)} %convolution_add_fusion.2, bf16[256,2048]{0,1:T(8,128)(2,1)} %collective-permute-done.2, bf16[2048,256]{1,0:T(8,128)(2,1)S(1)} %convolution_convert_fusion, bf16[256,7,256]{2,0,1:T(8,128)(2,1)} %param.8, pred[]{:T(512)} %bitcast.11), kind=kOutput, calls=%fused_computation.5 | convolution fusion | flops 538247168 | bytes 9568768 | tf_op jit(solution)/shard_map/dot_general | solution.py:23
  229.8 9.6 %collective-permute-done.5 = bf16[256,2048]{0,1:T(8,128)(2,1)} collective-permute-done((bf16[256,2048]{0,1:T(8,128)(2,1)}, bf16[256,2048]{0,1:T(8,128)(2,1)}, u32[]{:S(2)}, u32[]{:S(2)}) %collective-permute-start.5) | collective-permute-done | bytes 1048608 | tf_op jit(solution)/shard_map/ppermute | solution.py:10
  239.4 0.0 copy-start.1
  239.4 4.4 %fusion.24 = f32[256,2048]{1,0:T(8,128)} fusion(bf16[256,2048]{0,1:T(8,128)(2,1)} %collective-permute-done.5, bf16[2048,256]{1,0:T(8,128)(2,1)S(1)} %convolution_convert_fusion, bf16[256,7,256]{2,0,1:T(8,128)(2,1)} %param.8, pred[]{:T(512)} %bitcast.14), kind=kOutput, calls=%fused_computation.38 | convolution fusion | flops 537198592 | bytes 5374464 | tf_op jit(solution)/shard_map/dot_general | solution.py:23
  243.8 0.0 collective-permute-done.4
  243.8 0.0 copy-done.1
  243.8 4.6 %fusion.2 = bf16[256,2048]{1,0:T(8,128)(2,1)} fusion(f32[256,2048]{1,0:T(8,128)} %fusion.24, f32[256,2048]{1,0:T(8,128)S(1)} %copy-done.1, bf16[256,2048]{0,1:T(8,128)(2,1)} %collective-permute-done.4, bf16[2048,256]{1,0:T(8,128)(2,1)S(1)} %convolution_convert_fusion, bf16[256,7,256]{2,0,1:T(8,128)(2,1)} %param.8, pred[]{:T(512)} %bitcast.14), kind=kOutput, calls=%fused_computation.8 | convolution fusion | flops 538771456 | bytes 8520192 | tf_op jit(solution)/shard_map/dot_general | solution.py:23
  (8 shorter events, 0.1 us)
Async XLA Ops:
  6.5 106.4 %copy-start = (bf16[256,256]{1,0:T(8,128)(2,1)S(1)}, bf16[256,256]{1,0:T(8,128)(2,1)}, u32[]{:S(2)}) copy-start(bf16[256,256]{1,0:T(8,128)(2,1)} %param.7) | copy-start | bytes 393220
  11.8 21.9 %all-to-all-start = ((bf16[32,2,8,128]{3,2,1,0:T(8,128)(2,1)}), bf16[32,2,8,128]{3,2,1,0:T(8,128)(2,1)S(1)}, u32[]{:S(2)}, u32[]{:S(2)}) async-start(bf16[32,2,8,128]{3,2,1,0:T(8,128)(2,1)} %select_select_fusion), calls=%async_computation | async-start | bytes 262144 | tf_op jit(solution)/shard_map/all_to_all | solution.py:49
  24.4 88.6 %all-gather.2.cloned.1.call-start = ((), (), s32[]{:S(2)}) async-start(), calls=%async_computation.1 | async-start | bytes 1114112 | tf_op jit(solution)/shard_map/all_gather | solution.py:59
  114.7 47.7 %collective-permute-start.1 = (bf16[256,2048]{0,1:T(8,128)(2,1)S(1)}, bf16[256,2048]{0,1:T(8,128)(2,1)}, u32[]{:S(2)}, u32[]{:S(2)}) collective-permute-start(bf16[256,2048]{0,1:T(8,128)(2,1)S(1)} %bitcast.84), channel_id=1, source_target_pairs={{0,1},{1,2},{2,3},{3,4},{4,5},{5,6},{6,7},{7,8},{8,9},{9,10},{10,1... | collective-permute-start | bytes 3145736 | tf_op jit(solution)/shard_map/ppermute | solution.py:10
  116.6 48.3 %collective-permute-start = (bf16[256,2048]{0,1:T(8,128)(2,1)S(1)}, bf16[256,2048]{0,1:T(8,128)(2,1)}, u32[]{:S(2)}, u32[]{:S(2)}) collective-permute-start(bf16[256,2048]{0,1:T(8,128)(2,1)S(1)} %bitcast.85), channel_id=1, source_target_pairs={{0,15},{1,0},{2,1},{3,2},{4,3},{5,4},{6,5},{7,6},{8,7},{9,8},{10,9... | collective-permute-start | bytes 3145736 | tf_op jit(solution)/shard_map/ppermute | solution.py:10
  162.3 48.9 %collective-permute-start.3 = (bf16[256,2048]{0,1:T(8,128)(2,1)}, bf16[256,2048]{0,1:T(8,128)(2,1)}, u32[]{:S(2)}, u32[]{:S(2)}) collective-permute-start(bf16[256,2048]{0,1:T(8,128)(2,1)} %collective-permute-done.1), channel_id=1, source_target_pairs={{0,1},{1,2},{2,3},{3,4},{4,5},{5,6},{6,7},{7,8},{8,9},{9,10},{10,1... | collective-permute-start | bytes 3145736 | tf_op jit(solution)/shard_map/ppermute | solution.py:10
  164.9 53.1 %collective-permute-start.2 = (bf16[256,2048]{0,1:T(8,128)(2,1)}, bf16[256,2048]{0,1:T(8,128)(2,1)}, u32[]{:S(2)}, u32[]{:S(2)}) collective-permute-start(bf16[256,2048]{0,1:T(8,128)(2,1)} %collective-permute-done), channel_id=1, source_target_pairs={{0,15},{1,0},{2,1},{3,2},{4,3},{5,4},{6,5},{7,6},{8,7},{9,8},{10,9... | collective-permute-start | bytes 3145736 | tf_op jit(solution)/shard_map/ppermute | solution.py:10
  211.2 28.2 %collective-permute-start.5 = (bf16[256,2048]{0,1:T(8,128)(2,1)}, bf16[256,2048]{0,1:T(8,128)(2,1)}, u32[]{:S(2)}, u32[]{:S(2)}) collective-permute-start(bf16[256,2048]{0,1:T(8,128)(2,1)} %collective-permute-done.3), channel_id=1, source_target_pairs={{0,1},{1,2},{2,3},{3,4},{4,5},{5,6},{6,7},{7,8},{8,9},{9,10},{10,1... | collective-permute-start | bytes 3145736 | tf_op jit(solution)/shard_map/ppermute | solution.py:10
  218.1 25.8 %collective-permute-start.4 = (bf16[256,2048]{0,1:T(8,128)(2,1)}, bf16[256,2048]{0,1:T(8,128)(2,1)}, u32[]{:S(2)}, u32[]{:S(2)}) collective-permute-start(bf16[256,2048]{0,1:T(8,128)(2,1)} %collective-permute-done.2), channel_id=1, source_target_pairs={{0,15},{1,0},{2,1},{3,2},{4,3},{5,4},{6,5},{7,6},{8,7},{9,8},{10,9... | collective-permute-start | bytes 3145736 | tf_op jit(solution)/shard_map/ppermute | solution.py:10
  239.4 4.4 %copy-start.1 = (f32[256,2048]{1,0:T(8,128)S(1)}, f32[256,2048]{1,0:T(8,128)}, u32[]{:S(2)}) copy-start(f32[256,2048]{1,0:T(8,128)} %fusion.1) | copy-start | bytes 6291460
Sparse Core Ops, SparseCore 0:
  35.3 77.6 all-gather.1
where the time goes:
time: 256 us; the launch traced here: 255 us
  waiting for transfers between devices  174 us (68%)
  starting transfers between devices  30.1 us (12%)
  matrix products  30.1 us (12%)
  between operations  14.2 us (6%)
  other arithmetic  4.15 us (2%)
  local copies, waits for them, and re-layouts  2.74 us (1%)
    ppermute x6, waiting for transfers between devices, passed_along(): return lax.ppermute(value, axis, pairs)  87.2 us
    all_gather x1, waiting for transfers between devices, on_device(): lax.all_gather(needed, 'blk', axis=1, tiled=True)  77.8 us
    dot_general x7, matrix products, block_term(): return jnp.dot(masked_tile, source, preferred_element_type=jnp.float32)  28.4 us
    ppermute x6, starting transfers between devices, passed_along(): return lax.ppermute(value, axis, pairs)  17.5 us
    all_to_all x1, starting transfers between devices, on_device(): lax.all_to_all(outgoing, 'cluster', split_axis=0, concat_axis=0, tiled=True)  12.6 us
    all_to_all x1, waiting for transfers between devices, on_device(): lax.all_to_all(outgoing, 'cluster', split_axis=0, concat_axis=0, tiled=True)  9.07 us
  transfers between devices with their start and end apart: 8, of which 5 were waited for; matrix products, arithmetic and copies ran while one was open for 9% of the time, Pallas kernels for 0%

commit v1 on v0

--- a/solution.py
+++ b/solution.py
@@ -2,6 +2,13 @@
 import jax.numpy as jnp
 from jax import lax
 from jax.sharding import PartitionSpec as P
+
+
+def gather_over(value, axis, along):
+    size = lax.axis_size(axis)
+    tiles = jnp.stack([value for _ in range(size)])
+    tiles = lax.all_to_all(tiles, axis, split_axis=0, concat_axis=0)
+    return jnp.concatenate(tiles, axis=along)
 
 
 def passed_along(value, axis, steps):
@@ -55,9 +62,7 @@
     )
     needed = needed.reshape(list_len * num_funcs, my_columns)
     local_vals = jnp.dot(
-        basis_vals,
-        lax.all_gather(needed, "blk", axis=1, tiled=True),
-        preferred_element_type=jnp.float32,
+        basis_vals, gather_over(needed, "blk", 1), preferred_element_type=jnp.float32
     ).astype(jnp.bfloat16)
     norm_factor = local_vals.shape[1] ** (-0.5)
     my_reach = reach[0]

time: 256 us -> 220 us (0.86)
  the two profiles are of different devices: /device:TPU:114 before, /device:TPU:1 now
where the time goes in v1:
time: 220 us; the launch traced here: 219 us
  waiting for transfers between devices  115 us (52%)
  blocking collectives  34.4 us (16%)
  starting transfers between devices  34.1 us (16%)
  matrix products  28.7 us (13%)
  other arithmetic  3.52 us (2%)
  local copies, waits for them, and re-layouts  2.94 us (1%)
    ppermute x6, waiting for transfers between devices, passed_along(): return lax.ppermute(value, axis, pairs)  104 us
    all_to_all x1, blocking collectives, gather_over(): tiles = lax.all_to_all(tiles, axis, split_axis=0, concat_axis=0)  34.4 us
    dot_general x7, matrix products, block_term(): return jnp.dot(masked_tile, source, preferred_element_type=jnp.float32)  28.2 us
    ppermute x6, starting transfers between devices, passed_along(): return lax.ppermute(value, axis, pairs)  19.7 us
    all_to_all x1, starting transfers between devices, on_device(): lax.all_to_all(outgoing, 'cluster', split_axis=0, concat_axis=0, tiled=True)  14.4 us
    all_to_all x1, waiting for transfers between devices, on_device(): lax.all_to_all(outgoing, 'cluster', split_axis=0, concat_axis=0, tiled=True)  11.1 us
  transfers between devices with their start and end apart: 7, of which 6 were waited for; matrix products, arithmetic and copies ran while one was open for 11% of the time, Pallas kernels for 0%

profile of v1, /device:TPU:1, one launch (start us, length us, event | category | flops | bytes accessed | tf_op | source)
XLA Modules:
  0.0 219.4 jit_solution(9837043771213941112)
XLA Ops:
  0.0 0.0 copy-start
  0.0 0.8 broadcast_compare_fusion
  0.8 0.7 broadcast_subtract_fusion
  1.5 0.8 convert_reduce_fusion
  2.3 0.1 select_reduce_fusion
  2.4 0.1 copy.9
  2.5 0.1 fusion.70
  2.6 0.1 reshape.142
  2.8 0.1 copy.8
  2.9 0.1 copy.7
  3.0 1.5 gather_fusion
  4.4 0.9 select_select_fusion
  5.3 14.4 %all-to-all-start = ((bf16[32,2,8,128]{3,2,1,0:T(8,128)(2,1)}), bf16[32,2,8,128]{3,2,1,0:T(8,128)(2,1)S(1)}, u32[]{:S(2)}, u32[]{:S(2)}) async-start(bf16[32,2,8,128]{3,2,1,0:T(8,128)(2,1)} %select_select_fusion), calls=%async_computation | async-start | bytes 262144 | tf_op jit(solution)/shard_map/all_to_all | solution.py:56
  19.8 0.1 broadcast_in_dim.66
  19.8 0.1 broadcast_in_dim.67
  20.0 11.1 %all-to-all-done = bf16[32,2,8,128]{3,2,1,0:T(8,128)(2,1)S(1)} async-done(((bf16[32,2,8,128]{3,2,1,0:T(8,128)(2,1)}), bf16[32,2,8,128]{3,2,1,0:T(8,128)(2,1)S(1)}, u32[]{:S(2)}, u32[]{:S(2)}) %all-to-all-start) | async-done | bytes 131104 | tf_op jit(solution)/shard_map/all_to_all | solution.py:56
  31.1 0.6 gather_fusion.1
  31.8 0.1 broadcast_select_fusion
  31.9 0.1 copy.10
  32.0 0.1 stack.3
  32.1 34.4 %all_to_all.10 = bf16[16,256,128]{1,2,0:T(8,128)(2,1)S(1)} all-to-all(bf16[16,256,128]{1,2,0:T(8,128)(2,1)S(1)} %stack.3), channel_id=1, replica_groups=mesh['cluster'=32,'blk'=16] {'blk'}, dimensions={0} | all-to-all | bytes 2097152 | tf_op jit(solution)/shard_map/all_to_all | solution.py:10
  66.5 0.0 copy-done
  66.5 0.5 convolution_convert_fusion
  67.0 1.9 collective-permute-start.1
  68.9 5.5 %collective-permute-start = (bf16[256,2048]{0,1:T(8,128)(2,1)S(1)}, bf16[256,2048]{0,1:T(8,128)(2,1)}, u32[]{:S(2)}, u32[]{:S(2)}) collective-permute-start(bf16[256,2048]{0,1:T(8,128)(2,1)S(1)} %bitcast.88), channel_id=1, source_target_pairs={{0,15},{1,0},{2,1},{3,2},{4,3},{5,4},{6,5},{7,6},{8,7},{9,8},{10,9... | collective-permute-start | bytes 3145736 | tf_op jit(solution)/shard_map/ppermute | solution.py:17
  74.4 36.6 %collective-permute-done.1 = bf16[256,2048]{0,1:T(8,128)(2,1)} collective-permute-done((bf16[256,2048]{0,1:T(8,128)(2,1)S(1)}, bf16[256,2048]{0,1:T(8,128)(2,1)}, u32[]{:S(2)}, u32[]{:S(2)}) %collective-permute-start.1) | collective-permute-done | bytes 1048608 | tf_op jit(solution)/shard_map/ppermute | solution.py:17
  111.0 4.2 %collective-permute-start.3 = (bf16[256,2048]{0,1:T(8,128)(2,1)}, bf16[256,2048]{0,1:T(8,128)(2,1)}, u32[]{:S(2)}, u32[]{:S(2)}) collective-permute-start(bf16[256,2048]{0,1:T(8,128)(2,1)} %collective-permute-done.1), channel_id=1, source_target_pairs={{0,1},{1,2},{2,3},{3,4},{4,5},{5,6},{6,7},{7,8},{8,9},{9,10},{10,1... | collective-permute-start | bytes 3145736 | tf_op jit(solution)/shard_map/ppermute | solution.py:17
  115.8 24.9 %collective-permute-done = bf16[256,2048]{0,1:T(8,128)(2,1)} collective-permute-done((bf16[256,2048]{0,1:T(8,128)(2,1)S(1)}, bf16[256,2048]{0,1:T(8,128)(2,1)}, u32[]{:S(2)}, u32[]{:S(2)}) %collective-permute-start) | collective-permute-done | bytes 1048608 | tf_op jit(solution)/shard_map/ppermute | solution.py:17
  140.8 1.9 collective-permute-start.2
  142.7 2.2 %fusion.26 = f32[256,2048]{1,0:T(8,128)S(1)} fusion(bf16[2048,256]{1,0:T(8,128)(2,1)S(1)} %convolution_convert_fusion, bf16[256,7,256]{2,0,1:T(8,128)(2,1)} %param.8, pred[]{:T(512)} %bitcast), kind=kOutput, calls=%fused_computation.40 | convolution fusion | flops 537198592 | bytes 5374464 | tf_op jit(solution)/shard_map/dot_general | solution.py:30
  144.9 4.3 %convolution_add_fusion.3 = f32[256,2048]{1,0:T(8,128)} fusion(f32[256,2048]{1,0:T(8,128)S(1)} %fusion.26, bf16[256,2048]{0,1:T(8,128)(2,1)} %collective-permute-done, bf16[2048,256]{1,0:T(8,128)(2,1)S(1)} %convolution_convert_fusion, bf16[256,7,256]{2,0,1:T(8,128)(2,1)} %param.8, pred[]{:T(512)} %bitcast.9), kind=kOutput, calls=%fused_computation.7 | convolution fusion | flops 537722880 | bytes 7471616 | tf_op jit(solution)/shard_map/dot_general | solution.py:30
  149.2 7.3 %collective-permute-done.3 = bf16[256,2048]{0,1:T(8,128)(2,1)} collective-permute-done((bf16[256,2048]{0,1:T(8,128)(2,1)}, bf16[256,2048]{0,1:T(8,128)(2,1)}, u32[]{:S(2)}, u32[]{:S(2)}) %collective-permute-start.3) | collective-permute-done | bytes 1048608 | tf_op jit(solution)/shard_map/ppermute | solution.py:17
  156.5 4.2 %collective-permute-start.5 = (bf16[256,2048]{0,1:T(8,128)(2,1)}, bf16[256,2048]{0,1:T(8,128)(2,1)}, u32[]{:S(2)}, u32[]{:S(2)}) collective-permute-start(bf16[256,2048]{0,1:T(8,128)(2,1)} %collective-permute-done.3), channel_id=1, source_target_pairs={{0,1},{1,2},{2,3},{3,4},{4,5},{5,6},{6,7},{7,8},{8,9},{9,10},{10,1... | collective-permute-start | bytes 3145736 | tf_op jit(solution)/shard_map/ppermute | solution.py:17
  160.7 4.9 %convolution_add_fusion.2 = f32[256,2048]{1,0:T(8,128)} fusion(f32[256,2048]{1,0:T(8,128)} %convolution_add_fusion.3, bf16[256,2048]{0,1:T(8,128)(2,1)} %collective-permute-done.1, bf16[2048,256]{1,0:T(8,128)(2,1)S(1)} %convolution_convert_fusion, bf16[256,7,256]{2,0,1:T(8,128)(2,1)} %param.8, pred[]{:T(512)} %bitcast.9), kind=kOutput, calls=%fused_computation.6 | convolution fusion | flops 537722880 | bytes 7471616 | tf_op jit(solution)/shard_map/dot_general | solution.py:30
  165.6 23.8 %collective-permute-done.2 = bf16[256,2048]{0,1:T(8,128)(2,1)} collective-permute-done((bf16[256,2048]{0,1:T(8,128)(2,1)}, bf16[256,2048]{0,1:T(8,128)(2,1)}, u32[]{:S(2)}, u32[]{:S(2)}) %collective-permute-start.2) | collective-permute-done | bytes 1048608 | tf_op jit(solution)/shard_map/ppermute | solution.py:17
  189.5 1.9 collective-permute-start.4
  191.4 2.9 %fusion.25 = f32[256,2048]{1,0:T(8,128)S(1)} fusion(bf16[256,2048]{0,1:T(8,128)(2,1)} %collective-permute-done.3, bf16[2048,256]{1,0:T(8,128)(2,1)S(1)} %convolution_convert_fusion, bf16[256,7,256]{2,0,1:T(8,128)(2,1)} %param.8, pred[]{:T(512)} %bitcast.13), kind=kOutput, calls=%fused_computation.39 | convolution fusion | flops 537198592 | bytes 5374464 | tf_op jit(solution)/shard_map/dot_general | solution.py:30
  194.3 4.9 %fusion.1 = f32[256,2048]{1,0:T(8,128)} fusion(f32[256,2048]{1,0:T(8,128)S(1)} %fusion.25, f32[256,2048]{1,0:T(8,128)} %convolution_add_fusion.2, bf16[256,2048]{0,1:T(8,128)(2,1)} %collective-permute-done.2, bf16[2048,256]{1,0:T(8,128)(2,1)S(1)} %convolution_convert_fusion, bf16[256,7,256]{2,0,1:T(8,128)(2,1)} %param.8, pred[]{:T(512)} %bitcast.13), kind=kOutput, calls=%fused_computation.5 | convolution fusion | flops 538247168 | bytes 9568768 | tf_op jit(solution)/shard_map/dot_general | solution.py:30
  199.2 0.0 collective-permute-done.5
  199.2 0.0 copy-start.1
  199.2 4.4 %fusion.24 = f32[256,2048]{1,0:T(8,128)} fusion(bf16[256,2048]{0,1:T(8,128)(2,1)} %collective-permute-done.5, bf16[2048,256]{1,0:T(8,128)(2,1)S(1)} %convolution_convert_fusion, bf16[256,7,256]{2,0,1:T(8,128)(2,1)} %param.8, pred[]{:T(512)} %bitcast.16), kind=kOutput, calls=%fused_computation.38 | convolution fusion | flops 537198592 | bytes 5374464 | tf_op jit(solution)/shard_map/dot_general | solution.py:30
  203.6 11.2 %collective-permute-done.4 = bf16[256,2048]{0,1:T(8,128)(2,1)} collective-permute-done((bf16[256,2048]{0,1:T(8,128)(2,1)}, bf16[256,2048]{0,1:T(8,128)(2,1)}, u32[]{:S(2)}, u32[]{:S(2)}) %collective-permute-start.4) | collective-permute-done | bytes 1048608 | tf_op jit(solution)/shard_map/ppermute | solution.py:17
  214.8 0.0 copy-done.1
  214.8 4.6 %fusion.2 = bf16[256,2048]{1,0:T(8,128)(2,1)} fusion(f32[256,2048]{1,0:T(8,128)} %fusion.24, f32[256,2048]{1,0:T(8,128)S(1)} %copy-done.1, bf16[256,2048]{0,1:T(8,128)(2,1)} %collective-permute-done.4, bf16[2048,256]{1,0:T(8,128)(2,1)S(1)} %convolution_convert_fusion, bf16[256,7,256]{2,0,1:T(8,128)(2,1)} %param.8, pred[]{:T(512)} %bitcast.16), kind=kOutput, calls=%fused_computation.8 | convolution fusion | flops 538771456 | bytes 8520192 | tf_op jit(solution)/shard_map/dot_general | solution.py:30
  (8 shorter events, 0.1 us)
Async XLA Ops:
  0.0 66.5 %copy-start = (bf16[256,256]{1,0:T(8,128)(2,1)S(1)}, bf16[256,256]{1,0:T(8,128)(2,1)}, u32[]{:S(2)}) copy-start(bf16[256,256]{1,0:T(8,128)(2,1)} %param.7) | copy-start | bytes 393220
  5.3 25.8 %all-to-all-start = ((bf16[32,2,8,128]{3,2,1,0:T(8,128)(2,1)}), bf16[32,2,8,128]{3,2,1,0:T(8,128)(2,1)S(1)}, u32[]{:S(2)}, u32[]{:S(2)}) async-start(bf16[32,2,8,128]{3,2,1,0:T(8,128)(2,1)} %select_select_fusion), calls=%async_computation | async-start | bytes 262144 | tf_op jit(solution)/shard_map/all_to_all | solution.py:56
  67.0 44.0 %collective-permute-start.1 = (bf16[256,2048]{0,1:T(8,128)(2,1)S(1)}, bf16[256,2048]{0,1:T(8,128)(2,1)}, u32[]{:S(2)}, u32[]{:S(2)}) collective-permute-start(bf16[256,2048]{0,1:T(8,128)(2,1)S(1)} %bitcast.87), channel_id=1, source_target_pairs={{0,1},{1,2},{2,3},{3,4},{4,5},{5,6},{6,7},{7,8},{8,9},{9,10},{10,1... | collective-permute-start | bytes 3145736 | tf_op jit(solution)/shard_map/ppermute | solution.py:17
  68.9 71.8 %collective-permute-start = (bf16[256,2048]{0,1:T(8,128)(2,1)S(1)}, bf16[256,2048]{0,1:T(8,128)(2,1)}, u32[]{:S(2)}, u32[]{:S(2)}) collective-permute-start(bf16[256,2048]{0,1:T(8,128)(2,1)S(1)} %bitcast.88), channel_id=1, source_target_pairs={{0,15},{1,0},{2,1},{3,2},{4,3},{5,4},{6,5},{7,6},{8,7},{9,8},{10,9... | collective-permute-start | bytes 3145736 | tf_op jit(solution)/shard_map/ppermute | solution.py:17
  111.0 45.5 %collective-permute-start.3 = (bf16[256,2048]{0,1:T(8,128)(2,1)}, bf16[256,2048]{0,1:T(8,128)(2,1)}, u32[]{:S(2)}, u32[]{:S(2)}) collective-permute-start(bf16[256,2048]{0,1:T(8,128)(2,1)} %collective-permute-done.1), channel_id=1, source_target_pairs={{0,1},{1,2},{2,3},{3,4},{4,5},{5,6},{6,7},{7,8},{8,9},{9,10},{10,1... | collective-permute-start | bytes 3145736 | tf_op jit(solution)/shard_map/ppermute | solution.py:17
  140.8 48.7 %collective-permute-start.2 = (bf16[256,2048]{0,1:T(8,128)(2,1)}, bf16[256,2048]{0,1:T(8,128)(2,1)}, u32[]{:S(2)}, u32[]{:S(2)}) collective-permute-start(bf16[256,2048]{0,1:T(8,128)(2,1)} %collective-permute-done), channel_id=1, source_target_pairs={{0,15},{1,0},{2,1},{3,2},{4,3},{5,4},{6,5},{7,6},{8,7},{9,8},{10,9... | collective-permute-start | bytes 3145736 | tf_op jit(solution)/shard_map/ppermute | solution.py:17
  156.5 42.8 %collective-permute-start.5 = (bf16[256,2048]{0,1:T(8,128)(2,1)}, bf16[256,2048]{0,1:T(8,128)(2,1)}, u32[]{:S(2)}, u32[]{:S(2)}) collective-permute-start(bf16[256,2048]{0,1:T(8,128)(2,1)} %collective-permute-done.3), channel_id=1, source_target_pairs={{0,1},{1,2},{2,3},{3,4},{4,5},{5,6},{6,7},{7,8},{8,9},{9,10},{10,1... | collective-permute-start | bytes 3145736 | tf_op jit(solution)/shard_map/ppermute | solution.py:17
  189.5 25.3 %collective-permute-start.4 = (bf16[256,2048]{0,1:T(8,128)(2,1)}, bf16[256,2048]{0,1:T(8,128)(2,1)}, u32[]{:S(2)}, u32[]{:S(2)}) collective-permute-start(bf16[256,2048]{0,1:T(8,128)(2,1)} %collective-permute-done.2), channel_id=1, source_target_pairs={{0,15},{1,0},{2,1},{3,2},{4,3},{5,4},{6,5},{7,6},{8,7},{9,8},{10,9... | collective-permute-start | bytes 3145736 | tf_op jit(solution)/shard_map/ppermute | solution.py:17
  199.2 15.5 %copy-start.1 = (f32[256,2048]{1,0:T(8,128)S(1)}, f32[256,2048]{1,0:T(8,128)}, u32[]{:S(2)}) copy-start(f32[256,2048]{1,0:T(8,128)} %fusion.1) | copy-start | bytes 6291460
